TPU v7x, 128 devices: a whole 4x4x4 slice. The times are simulated.
128 devices in a mesh: grp: 32 (over x, z_lo, y), seq: 4 (over z_hi, core).
Axes of the slice: x: 4, y: 4, z: 4 (z_hi: 2, z_lo: 2; z = z_hi * 2 + z_lo), core: 2. Of those that a mesh axis runs over, the one named last changes fastest.
Arguments:
- x_home: bfloat16 [65536, 512], P(('grp', 'seq')), may hold values from -6 to 6
- dy_home: bfloat16 [65536, 512], P(('grp', 'seq')), may hold values from -6 to 6
- w_in: bfloat16 [512, 2048], replicated, may hold values from -0.25 to 0.25
- w_out: bfloat16 [512, 512], replicated, may hold values from -0.25 to 0.25
- place: int32 [32, 4, 512], P('grp', 'seq'), may hold values from 0 to 511, each once within a row
- seg_ids: int32 [32, 2048], P('grp'), may hold values from 0 to 1, as said below
Outputs:
- dx_home: bfloat16 [65536, 512], P(('grp', 'seq'))
- grad_w_in: float32 [512, 2048], replicated
- grad_w_out: float32 [512, 512], replicated
Inputs may be any that keep to these rules, and one draw needn't show every extreme that they name: `place`: each device's list names each of its 512 received events once. `seg_ids`: history numbers never fall along a device set; every set has 2 histories, one of exactly 1536 events and one of 512 events, in either order.
All inputs are finite; a program needn't handle non-finite values.
Results may differ from a plain program's by a relative error of at most 0.0075.
Values may be sent and summed in bfloat16 or wider, within the bound.
A program may use at most 192 MiB of HBM per device.

v0:
```python
import jax
import jax.numpy as jnp
from jax import lax
from jax.experimental import pallas as pl
from jax.experimental.pallas import tpu as pltpu
from jax.sharding import PartitionSpec as P

BF = jnp.bfloat16
F32 = jnp.float32
MESH = pl.DeviceIdType.MESH
NN = (((1,), (0,)), ((), ()))
NT = (((1,), (1,)), ((), ()))
TN = (((0,), (0,)), ((), ()))


def mm(a, b, dims=NN):
    return lax.dot_general(a, b, dims, preferred_element_type=F32)


def remote(src, dst, send, recv, device):
    return pltpu.make_async_remote_copy(
        src_ref=src,
        dst_ref=dst,
        send_sem=send,
        recv_sem=recv,
        device_id=device,
        device_id_type=MESH,
    )


def wait_for(ref, sem):
    pltpu.make_async_copy(ref, ref, sem).wait()


def kernel(
    x_ref, dy_ref, win_ref, wout_ref, place_ref, seg_ref,
    dx_out, gin_out, gout_out,
    rows, perm, x_all, dy_all, act, slope, qm, qn, kn, vn, wc, fc, out_u, dm_t, stats,
    dom, don, dv_u, dk_u, dpre, wsl, wt, wo, places,
    ge_s, ge_r, gl_s, gl_r, ag, dxs, dxp, zr, fin,
    local_sem, plane_s, plane_r, z_s, z_r, core_s, core_r, seq_s, seq_r, ge_sem, gl_sem,
    ag_s, ag_r, dxc_s, dxc_r, dxz_s, dxz_r, home_sem,
):
    g = lax.axis_index("grp")
    s = lax.axis_index("seq")
    x, zl, y = g // 8, (g // 4) % 2, g % 4
    zh, c = s // 2, s % 2
    xy = x * 4 + y

    def grp(x_, zl_, y_):
        return (x_ * 2 + zl_) * 4 + y_

    weight_copies = []
    for b in range(4):
        weight_copies.append(
            pltpu.make_async_copy(
                win_ref.at[:, pl.ds(pl.multiple_of(b * 512 + s * 128, 128), 128)],
                wsl.at[:, b * 128 : (b + 1) * 128],
                local_sem.at[b],
            )
        )
    weight_copies.append(
        pltpu.make_async_copy(
            wout_ref.at[pl.ds(pl.multiple_of(s * 128, 128), 128)], wo, local_sem.at[4]
        )
    )
    for copy in weight_copies:
        copy.start()

    barrier = pltpu.get_barrier_semaphore()

    @pl.loop(1, 32)
    def _(i):
        pl.semaphore_signal(
            barrier, inc=1, device_id=(lax.rem(g + i, 32), s), device_id_type=MESH
        )

    for i in range(1, 4):
        pl.semaphore_signal(
            barrier, inc=1, device_id=(g, lax.rem(s + i, 4)), device_id_type=MESH
        )
    pl.semaphore_signal(
        barrier, inc=1, device_id=(grp(x, 1 - zl, y), (1 - zh) * 2 + c), device_id_type=MESH
    )
    pl.semaphore_wait(barrier, 35)

    homes = (x_ref, dy_ref)
    for a in range(2):

        @pl.loop(1, 16)
        def _(i, a=a):
            to = lax.rem(xy + i, 16)
            tx, ty = to // 4, lax.rem(to, 4)
            remote(
                homes[a].at[tx, :, ty],
                rows.at[a, c, pl.ds(zl, 2), zh, xy],
                plane_s.at[a],
                plane_r.at[a],
                (grp(tx, zl, ty), s),
            ).start()

        pltpu.make_async_copy(
            homes[a].at[x, :, y], rows.at[a, c, pl.ds(zl, 2), zh, xy], plane_r.at[a]
        ).start()
        if a == 0:
            pltpu.make_async_copy(place_ref, places.at[s], local_sem.at[5]).start()
            for i in range(1, 4):
                remote(
                    place_ref,
                    places.at[s],
                    seq_s.at[0, i - 1],
                    seq_r.at[0, i - 1],
                    (g, lax.rem(s + i, 4)),
                ).start()

    z_peers = (
        (grp(x, 1 - zl, y), s),
        (grp(x, 1 - zl, y), (1 - zh) * 2 + c),
        (g, (1 - zh) * 2 + c),
    )

    def plane_done(a):
        return rows.at[a, c, pl.ds(zl, 2), zh]

    def block(a, core, zl_, zh_):
        return rows.at[a, core, 2 * zl_, zh_]

    def z_out(a, k):
        src = rows.at[a, c, 1, zh] if k < 2 else block(a, c, zl, zh)
        return remote(
            src, block(a, c, zl, zh), z_s.at[a, k], z_r.at[a, k], z_peers[k]
        )

    where_from = ((1 - zl, zh), (1 - zl, 1 - zh), (zl, 1 - zh), (zl, zh))

    def core_out(a, k):
        ref = block(a, c, *where_from[k])
        return remote(ref, ref, core_s.at[a, k], core_r.at[a, k], (g, zh * 2 + 1 - c))

    def spread_plane(a):
        wait_for(plane_done(a), plane_r.at[a])
        for k in range(3):
            z_out(a, k).start()
        core_out(a, 3).start()

    def forward(a):
        for k in range(3):
            wait_for(block(a, c, *where_from[k]), z_r.at[a, k])
            core_out(a, k).start()

    def from_core(a):
        for k in range(4):
            wait_for(block(a, 1 - c, *where_from[k]), core_r.at[a, k])

    for copy in weight_copies:
        copy.wait()
    wt[...] = wsl[...].T
    spread_plane(0)

    wait_for(places.at[0], local_sem.at[5])
    for i in range(1, 4):
        wait_for(places.at[0], seq_r.at[0, i - 1])

    def slot_of(p):
        return ((p >> 6) & 1) * 256 + (p >> 7) * 64 + (p & 63)

    @pl.loop(0, 4)
    def _(q):
        slot = slot_of(places[q])
        column = jnp.broadcast_to(slot.astype(F32), (128, 512)).T
        lane = lax.broadcasted_iota(jnp.int32, (512, 128), 1).astype(F32)
        for b in range(4):
            perm[q, :, b * 128 : (b + 1) * 128] = jnp.where(
                column == lane + float(b * 128), 1.0, 0.0
            ).astype(BF)

    def ordered(a, q):
        low = rows[a, lax.rem(q, 2), 0, q // 2].reshape(256, 512)
        high = rows[a, lax.rem(q, 2), 2, q // 2].reshape(256, 512)
        return (mm(perm[q, :, :256], low) + mm(perm[q, :, 256:], high)).astype(BF)

    spread_plane(1)
    forward(0)
    from_core(0)

    @pl.loop(0, 4)
    def _(q):
        x_all[q] = ordered(0, q)
        for b in range(4):
            pre = mm(wt[b * 128 : (b + 1) * 128, :], x_all[q], NT)
            sig = 0.5 * jnp.tanh(0.5 * pre) + 0.5
            full = pre * sig
            slope[q, b * 128 : (b + 1) * 128, :] = sig + full * (1.0 - sig)
            cut = full.astype(BF)
            act[q, b * 128 : (b + 1) * 128, :] = cut
            if b == 1:
                vn[q] = cut.T
            if b == 2:
                qn[q] = (cut * BF(0.125)).T
                scaled = cut * BF(0.0625)
                zero = jnp.zeros((64, 512), BF)
                qm[q, 0] = jnp.concatenate([scaled[:64], zero], axis=0)
                qm[q, 1] = jnp.concatenate([zero, scaled[64:]], axis=0)
            if b == 3:
                kn[q] = cut.T

    forward(1)

    is_a = seg_ref[0, 0] == seg_ref[0, 1535]
    in_a = jnp.where(is_a, 1.0, 0.0).astype(F32)
    in_b = 1.0 - in_a
    long, short = 1.0 / 1536.0, 1.0 / 512.0
    inv_len = (
        in_a * long + in_b * short, long, long, in_a * short + in_b * long
    )

    def query_of(f):
        return jnp.where(f == 2, 2, jnp.where(is_a, f + 1, 3))

    def key_of(f):
        return jnp.where(f == 2, 1, jnp.where(is_a, 0, 2 - f))

    def causal(rows_, cols):
        return lax.broadcasted_iota(jnp.int32, (rows_, cols), 0) <= lax.broadcasted_iota(
            jnp.int32, (rows_, cols), 1
        )

    def weigh(u, qi, ki, head, half, first, masked):
        keys = pl.ds(half * 256, 256)
        h = mm(kn[ki, keys, :], qm[qi, head, :, first:])
        t = jnp.tanh(h)
        a = 1.0 + t
        w = h * a
        f = a * (1.0 - w) + (w + w)
        if masked:
            keep = causal(256, 512 - first)
            w = jnp.where(keep, w, 0.0)
            f = jnp.where(keep, f, 0.0)
        w = w.astype(BF)
        wc[u, head, keys, first:] = w
        fc[u, head, keys, first:] = f.astype(BF)
        return mm(act[ki, 128 + head * 64 : 192 + head * 64, keys], w)

    @pl.loop(0, 4)
    def _(q):
        for head in range(2):
            lanes = slice(head * 64, head * 64 + 64)
            out_u[q, lanes, :] = weigh(q, q, q, head, 0, 0, True)
            out_u[q, lanes, 256:] += weigh(q, q, q, head, 1, 256, True)

    @pl.loop(0, 3)
    def _(f):
        qi, ki = query_of(f), key_of(f)
        for head in range(2):
            lanes = slice(head * 64, head * 64 + 64)
            out_u[4 + f, lanes, :] = weigh(4 + f, qi, ki, head, 0, 0, False) + weigh(
                4 + f, qi, ki, head, 1, 0, False
            )

    from_core(1)

    @pl.loop(0, 4)
    def _(q):
        dy_all[q] = ordered(1, q)
        dm_t[q] = mm(wo[...], dy_all[q], NT)

    for q in range(4):
        total = out_u[q]
        if q == 1:
            total = total + in_a * out_u[4]
        if q == 2:
            total = total + out_u[6] + in_a * out_u[5]
        if q == 3:
            total = total + in_b * (out_u[4] + out_u[5])
        total = total * inv_len[q]
        out_u[q] = total
        centre = jnp.mean(total, axis=0, keepdims=True)
        away = total - centre
        d_normed = dm_t[q] * act[q, :128, :].astype(F32)
        stats[s, 0, q : q + 1, :] = centre
        stats[s, 1, q : q + 1, :] = jnp.sum(away * away, axis=0, keepdims=True)
        stats[s, 2, q : q + 1, :] = jnp.sum(d_normed, axis=0, keepdims=True)
        stats[s, 3, q : q + 1, :] = jnp.sum(d_normed * away, axis=0, keepdims=True)

    def stats_out(i):
        return remote(
            stats.at[s], stats.at[s], seq_s.at[1, i - 1], seq_r.at[1, i - 1],
            (g, lax.rem(s + i, 4)),
        )

    for i in range(1, 4):
        stats_out(i).start()
    for i in range(1, 4):
        wait_for(stats.at[lax.rem(s + i, 4)], seq_r.at[1, 3 - i])

    centres = [stats[r, 0] for r in range(4)]
    mean_all = (centres[0] + centres[1] + centres[2] + centres[3]) * 0.25
    square = jnp.zeros_like(mean_all)
    plain = jnp.zeros_like(mean_all)
    cross = jnp.zeros_like(mean_all)
    for r in range(4):
        off = centres[r] - mean_all
        square += stats[r, 1] + 128.0 * off * off
        plain += stats[r, 2]
        cross += stats[r, 3] + off * stats[r, 2]
    spread_all = lax.rsqrt(square * (1.0 / 512.0) + 1e-5)
    plain = plain * (1.0 / 512.0)
    cross = cross * spread_all * (1.0 / 512.0)

    grad_out = jnp.zeros((128, 512), F32)
    grad_u = jnp.zeros((128, 512), F32)
    for q in range(4):
        gate = act[q, :128, :].astype(F32)
        spread = spread_all[q : q + 1]
        normed = (out_u[q] - mean_all[q : q + 1]) * spread
        d_mixed = dm_t[q]
        mixed = (normed * gate).astype(BF)
        d_u = (d_mixed * normed * slope[q, :128, :]).astype(BF)
        dpre[q, :128, :] = d_u
        d_out = (
            (d_mixed * gate - plain[q : q + 1] - normed * cross[q : q + 1])
            * (spread * (0.5 * inv_len[q]))
        ).astype(BF)
        zero = jnp.zeros((64, 512), BF)
        dom[q, 0] = jnp.concatenate([d_out[:64], zero], axis=0)
        dom[q, 1] = jnp.concatenate([zero, d_out[64:]], axis=0)
        don[q] = d_out.T
        grad_out += mm(mixed, dy_all[q])
        grad_u += mm(d_u, x_all[q])

    def grads_out(buf, got, sem):
        @pl.loop(1, 32)
        def _(i):
            to = lax.rem(g + i, 32)
            remote(buf.at[to], got.at[g], sem.at[0], sem.at[1], (to, s)).start()

        pltpu.make_async_copy(buf.at[g], got.at[g], sem.at[1]).start()

    ge_s[:, 0] = grad_u.T.astype(BF).reshape(32, 16, 128)
    for b in range(4):
        ge_s[8 * b : 8 * b + 8, 1] = (
            grad_out[:, b * 128 : (b + 1) * 128].astype(BF).reshape(8, 16, 128)
        )
    grads_out(ge_s, ge_r, ge_sem)

    def attend_back(u, qi, ki, masked):
        lane = lax.broadcasted_iota(jnp.int32, (256, 128), 1)
        d_q = [None, None]
        for half in range(2):
            keys = pl.ds(half * 256, 256)
            first = 256 if masked and half == 1 else 0
            d_v, d_k = [], []
            for head in range(2):
                d_w = mm(vn[ki, keys, :], dom[qi, head, :, first:])
                d_s = (d_w * fc[u, head, keys, first:].astype(F32)).astype(BF)
                d_v.append(mm(wc[u, head, keys, first:], don[qi, first:, :]))
                d_k.append(mm(d_s, qn[qi, first:, :]))
                part = mm(act[ki, 384 + head * 64 : 448 + head * 64, keys], d_s)
                lanes = slice(head * 64, head * 64 + 64)
                if half == 0:
                    out_u[u, lanes, :] = part
                else:
                    out_u[u, lanes, first:] += part
            dv_u[u, keys, :] = jnp.where(lane < 64, d_v[0], d_v[1])
            dk_u[u, keys, :] = jnp.where(lane < 64, d_k[0], d_k[1])

    @pl.loop(0, 4)
    def _(q):
        attend_back(q, q, q, True)

    @pl.loop(0, 3)
    def _(f):
        attend_back(4 + f, query_of(f), key_of(f), False)

    for q in range(4):
        d_q, d_k, d_v = out_u[q], dk_u[q], dv_u[q]
        if q == 0:
            d_k = d_k + in_a * (dk_u[4] + dk_u[5])
            d_v = d_v + in_a * (dv_u[4] + dv_u[5])
        if q == 1:
            d_q = d_q + in_a * out_u[4]
            d_k = d_k + dk_u[6] + in_b * dk_u[5]
            d_v = d_v + dv_u[6] + in_b * dv_u[5]
        if q == 2:
            d_q = d_q + out_u[6] + in_a * out_u[5]
            d_k = d_k + in_b * dk_u[4]
            d_v = d_v + in_b * dv_u[4]
        if q == 3:
            d_q = d_q + in_b * (out_u[4] + out_u[5])
        dpre[q, 128:256, :] = (2.0 * d_v.T * slope[q, 128:256, :]).astype(BF)
        dpre[q, 256:384, :] = (0.125 * d_q * slope[q, 256:384, :]).astype(BF)
        dpre[q, 384:512, :] = (d_k.T * slope[q, 384:512, :]).astype(BF)

    def partial(q):
        return mm(dpre[q], wt[...], TN)

    def dx_core(k):
        return remote(
            dxs.at[k], dxp.at[k], dxc_s.at[k], dxc_r.at[k], (g, zh * 2 + 1 - c)
        )

    for k in range(2):
        dxs[k] = partial(2 * k + 1 - c).astype(BF)
        dx_core(k).start()

    for b in range(1, 4):
        total = jnp.zeros((128, 512), F32)
        for q in range(4):
            total += mm(dpre[q, b * 128 : (b + 1) * 128, :], x_all[q])
        gl_s[:, b - 1] = total.T.astype(BF).reshape(32, 16, 128)

    def dx_z(k, src):
        return remote(src, zr.at[k], dxz_s.at[k], dxz_r.at[k], z_peers[k])

    for k in range(2):
        k_zh = lax.rem(zh + 1 + k, 2)
        q = k_zh * 2 + c
        mine = partial(q)
        mine = mine + jnp.where(q == s, 1.0, 0.0) * dy_all[q].astype(F32)
        wait_for(dxp.at[k_zh], dxc_r.at[k_zh])
        both = (mine + dxp[k_zh].astype(F32)).astype(BF)
        slot = slot_of(places[q])
        back = jnp.where(
            lax.broadcasted_iota(jnp.int32, (512, 512), 0) == slot, 1.0, 0.0
        ).astype(BF)
        dxs[2 + k] = mm(back, both).astype(BF)
        half_mine = pl.ds(pl.multiple_of(zl * 256, 256), 256)
        half_other = pl.ds(pl.multiple_of((1 - zl) * 256, 256), 256)
        if k == 0:
            dx_z(2, dxs.at[2, half_mine]).start()
            dx_z(1, dxs.at[2, half_other]).start()
        else:
            dx_z(0, dxs.at[3, half_other]).start()

    grads_out(gl_s, gl_r, gl_sem)

    for k in range(3):
        wait_for(zr.at[k], dxz_r.at[k])
    own = (
        dxs[3, pl.ds(pl.multiple_of(zl * 256, 256), 256)].astype(F32) + zr[2].astype(F32)
    ).astype(BF)
    other = (zr[0].astype(F32) + zr[1].astype(F32)).astype(BF)
    fin[pl.ds(zl, 1)] = own.reshape(1, 16, 16, 512)
    fin[pl.ds(1 - zl, 1)] = other.reshape(1, 16, 16, 512)

    @pl.loop(1, 16)
    def _(i):
        to = lax.rem(xy + i, 16)
        tx, ty = to // 4, lax.rem(to, 4)
        remote(
            fin.at[:, to], dx_out.at[x, :, y], home_sem.at[0], home_sem.at[1],
            (grp(tx, zl, ty), s),
        ).start()

    pltpu.make_async_copy(fin.at[:, xy], dx_out.at[x, :, y], home_sem.at[1]).start()

    first = jnp.where(c == 0, x, y)
    second = jnp.where(c == 0, y, x)
    zz = zl * 2 + zh
    wait_for(ge_r, ge_sem.at[1])
    wait_for(gl_r, gl_sem.at[1])
    early = jnp.sum(ge_r[...].astype(F32), axis=0)
    late = jnp.sum(gl_r[...].astype(F32), axis=0)
    here = ag.at[c, first, second, zz]
    here[0:1] = early[0:1].astype(BF)
    here[1:4] = late.astype(BF)
    here[4:5] = early[1:2].astype(BF)

    def spread_ag(phase, ref, peers):
        copies = [
            remote(ref, ref, ag_s.at[phase, k], ag_r.at[phase, k], peer)
            for k, peer in enumerate(peers)
        ]
        for copy in copies:
            copy.start()
        for k in range(len(peers)):
            wait_for(ref, ag_r.at[phase, k])
        return copies

    def along(i, on_first):
        nf = lax.rem(first + i, 4) if on_first else first
        ns = second if on_first else lax.rem(second + i, 4)
        nx = jnp.where(c == 0, nf, ns)
        ny = jnp.where(c == 0, ns, nf)
        return (grp(nx, zl, ny), s)

    ag_copies = spread_ag(0, here, z_peers)
    ag_copies += spread_ag(
        1, ag.at[c, first, second], [along(i, False) for i in range(1, 4)]
    )
    ag_copies += spread_ag(2, ag.at[c, first], [along(i, True) for i in range(1, 4)])
    ag_copies += spread_ag(3, ag.at[c], [(g, zh * 2 + 1 - c)])

    factor = 1.0 / 256.0
    for cc in range(2):
        for z in range(4):
            zl_, zh_ = z // 2, z % 2
            s_ = zh_ * 2 + cc
            for x_ in range(4):

                @pl.loop(0, 4)
                def _(y_, cc=cc, z=z, x_=x_, zl_=zl_, s_=s_):
                    f_, n_ = (x_, y_) if cc == 0 else (y_, x_)
                    group = grp(x_, zl_, y_)
                    at = pl.ds(pl.multiple_of(group * 16, 16), 16)
                    for b in range(4):
                        lo = b * 512 + s_ * 128
                        gin_out[at, lo : lo + 128] = ag[cc, f_, n_, z, b].astype(F32) * factor
                    at = pl.ds(pl.multiple_of(s_ * 128 + (zl_ * 4 + y_) * 16, 16), 16)
                    gout_out[at, x_ * 128 : x_ * 128 + 128] = (
                        ag[cc, f_, n_, z, 4].astype(F32) * factor
                    )

    wait_for(dx_out, home_sem.at[1])
    wait_for(fin.at[:, 0:15], home_sem.at[0])
    for copy in ag_copies:
        copy.wait_send()
    for a in range(2):
        wait_for(rows.at[a, c, 0:2, 0, 0:15], plane_s.at[a])
        for k in range(3):
            z_out(a, k).wait_send()
        for k in range(4):
            core_out(a, k).wait_send()
    for i in range(1, 4):
        wait_for(places.at[0], seq_s.at[0, i - 1])
        stats_out(i).wait_send()
    for k in range(2):
        dx_core(k).wait_send()
    for k in range(3):
        wait_for(zr.at[k], dxz_s.at[k])
    wait_for(ge_s.at[0:31], ge_sem.at[0])
    wait_for(gl_s.at[0:31], gl_sem.at[0])


def per_device(x_home, dy_home, w_in, w_out, place, seg_ids):
    shape = (4, 2, 4, 16, 512)
    vm = pltpu.VMEM
    dma = pltpu.SemaphoreType.DMA
    hbm = pl.BlockSpec(memory_space=pl.ANY)
    in_vmem = pl.BlockSpec(memory_space=pltpu.VMEM)
    dx, g_in, g_out = pl.pallas_call(
        kernel,
        out_shape=(
            jax.ShapeDtypeStruct(shape, BF),
            jax.ShapeDtypeStruct((512, 2048), F32),
            jax.ShapeDtypeStruct((512, 512), F32),
        ),
        in_specs=[
            hbm, hbm, hbm, hbm, in_vmem, pl.BlockSpec(memory_space=pltpu.SMEM),
        ],
        out_specs=(hbm, in_vmem, in_vmem),
        scratch_shapes=[
            vm((2, 2, 3, 2, 16, 16, 512), BF),
            vm((4, 512, 512), BF),
            vm((4, 512, 512), BF),
            vm((4, 512, 512), BF),
            vm((4, 512, 512), BF),
            vm((4, 512, 512), F32),
            vm((4, 2, 128, 512), BF),
            vm((4, 512, 128), BF),
            vm((4, 512, 128), BF),
            vm((4, 512, 128), BF),
            vm((7, 2, 512, 512), BF),
            vm((7, 2, 512, 512), BF),
            vm((7, 128, 512), F32),
            vm((4, 128, 512), F32),
            vm((4, 4, 4, 512), F32),
            vm((4, 2, 128, 512), BF),
            vm((4, 512, 128), BF),
            vm((7, 512, 128), F32),
            vm((7, 512, 128), F32),
            vm((4, 512, 512), BF),
            vm((512, 512), BF),
            vm((512, 512), BF),
            vm((128, 512), BF),
            vm((4, 1, 512), jnp.int32),
            vm((32, 2, 16, 128), BF),
            vm((32, 2, 16, 128), BF),
            vm((32, 3, 16, 128), BF),
            vm((32, 3, 16, 128), BF),
            vm((2, 4, 4, 4, 5, 16, 128), BF),
            vm((4, 512, 512), BF),
            vm((2, 512, 512), BF),
            vm((3, 256, 512), BF),
            vm((2, 16, 16, 512), BF),
            dma((6,)), dma((2,)), dma((2,)), dma((2, 3)), dma((2, 3)), dma((2, 4)),
            dma((2, 4)), dma((2, 3)), dma((2, 3)), dma((2,)), dma((2,)),
            dma((4, 3)), dma((4, 3)), dma((2,)), dma((2,)), dma((3,)), dma((3,)), dma((2,)),
        ],
        compiler_params=pltpu.CompilerParams(
            collective_id=0, has_side_effects=True, vmem_limit_bytes=63 * 2**20
        ),
    )(
        x_home.reshape(shape),
        dy_home.reshape(shape),
        w_in,
        w_out,
        place.reshape(1, 512),
        seg_ids.reshape(1, 2048),
    )
    return dx.reshape(512, 512), g_in, g_out


def solution(mesh):
    in_specs = (
        P(("grp", "seq"), None),
        P(("grp", "seq"), None),
        P(),
        P(),
        P("grp", "seq", None),
        P("grp", None),
    )
    out_specs = (P(("grp", "seq"), None), P(), P())
    return jax.shard_map(
        per_device, mesh=mesh, in_specs=in_specs, out_specs=out_specs, check_vma=False
    )
```

profile of v0, /device:TPU:1, one launch (start us, length us, event | category | flops | bytes accessed | tf_op | source)
XLA Modules:
  0.0 124.6 jit_solution(5270408966957473892)
XLA Ops:
  0.6 116.3 %shard_map.85 = (bf16[4,2,4,16,512]{4,3,2,1,0:T(8,128)(2,1)}, f32[512,2048]{1,0:T(8,128)}, f32[512,512]{1,0:T(8,128)}) custom-call(bf16[4,2,4,16,512]{4,3,2,1,0:T(8,128)(2,1)} %bitcast.4, bf16[4,2,4,16,512]{4,3,2,1,0:T(8,128)(2,1)} %bitcast.5, bf16[512,2048]{1,0:T(8,128)(2,1)} %win_ref.1, bf16[512,512]{1,0:T(8,128)(2,1)} %wout_ref.1, s32[1,512]{1,0:T(1,128)} %bitcast.7, ...), custom_call_target="tpu_custom_call" | custom-call | tf_op jit(solution)/shard_map/pallas_call | solution.py:541
  117.0 1.9 %copy.12 = bf16[512,512]{1,0:T(8,128)(2,1)} copy(bf16[512,512]{1,0:T(8,128)(2,1)} %bitcast.6) | data formatting | bytes 1048576
  118.8 0.0 copy-start
  118.9 4.8 %copy.13 = f32[512,2048]{1,0:T(8,128)} copy(f32[512,2048]{1,0:T(8,128)} %get-tuple-element.13) | data formatting | bytes 8388608
  123.6 0.0 copy-done
  123.6 1.0 copy.14
Async XLA Ops:
  118.8 4.8 %copy-start = (f32[512,512]{1,0:T(8,128)S(1)}, f32[512,512]{1,0:T(8,128)}, u32[]{:S(2)}) copy-start(f32[512,512]{1,0:T(8,128)} %get-tuple-element.14) | copy-start | bytes 3145732
where the time goes:
time: 125 us
  Pallas kernels  116 us (93%)
  local copies, waits for them, and re-layouts  7.63 us (6%)
    pallas_call x1, Pallas kernels, per_device(): pl.pallas_call(kernel, out_shape=(jax.ShapeDtypeStruct(shape, BF), jax.Sh...  116 us
    unnamed x5, local copies, waits for them, and re-layouts  7.63 us

commit v1 on v0

v1 whole, which is shorter than its diff:
```python
import jax
import jax.numpy as jnp
from jax import lax
from jax.experimental import pallas as pl
from jax.experimental.pallas import tpu as pltpu
from jax.sharding import PartitionSpec as P

BF = jnp.bfloat16
F32 = jnp.float32
MESH = pl.DeviceIdType.MESH
NN = (((1,), (0,)), ((), ()))
NT = (((1,), (1,)), ((), ()))
TN = (((0,), (0,)), ((), ()))


def mm(a, b, dims=NN):
    return lax.dot_general(a, b, dims, preferred_element_type=F32)


def remote(src, dst, send, recv, device):
    return pltpu.make_async_remote_copy(
        src_ref=src,
        dst_ref=dst,
        send_sem=send,
        recv_sem=recv,
        device_id=device,
        device_id_type=MESH,
    )


def wait_for(ref, sem):
    pltpu.make_async_copy(ref, ref, sem).wait()


def kernel(
    x_ref, dy_ref, win_ref, wout_ref, place_ref, seg_ref,
    dx_out, age, agl,
    rows, perm, x_all, dy_all, act, slope, qm, qn, kn, vn, wc, fc, out_u, dm_t, stats,
    dom, don, dv_u, dk_u, dpre, wsl, wt, wo, places,
    ge_s, ge_r, gl_s, gl_r, met_e, mine_e, met_l, mine_l, acc, dxs, dxp, zr, fin,
    local_sem, plane_s, plane_r, z_s, z_r, core_s, core_r, seq_s, seq_r, ge_sem, gl_sem,
    ag_s, ag_r, ag_l, dxc_s, dxc_r, dxz_s, dxz_r, home_sem,
):
    g = lax.axis_index("grp")
    s = lax.axis_index("seq")
    x, zl, y = g // 8, (g // 4) % 2, g % 4
    zh, c = s // 2, s % 2

    def grp(x_, zl_, y_):
        return (x_ * 2 + zl_) * 4 + y_

    weight_copies = []
    for b in range(4):
        weight_copies.append(
            pltpu.make_async_copy(
                win_ref.at[:, pl.ds(pl.multiple_of(b * 512 + s * 128, 128), 128)],
                wsl.at[:, b * 128 : (b + 1) * 128],
                local_sem.at[b],
            )
        )
    weight_copies.append(
        pltpu.make_async_copy(
            wout_ref.at[pl.ds(pl.multiple_of(s * 128, 128), 128)], wo, local_sem.at[4]
        )
    )
    for copy in weight_copies:
        copy.start()

    barrier = pltpu.get_barrier_semaphore()

    def shifted(i, sign):
        return lax.rem(x + 4 + sign * (i // 4), 4), lax.rem(y + 4 + sign * lax.rem(i, 4), 4)

    @pl.loop(1, 16)
    def _(i):
        tx, ty = shifted(i, 1)
        pl.semaphore_signal(
            barrier, inc=1, device_id=(grp(tx, zl, ty), s), device_id_type=MESH
        )

    for i in range(1, 4):
        pl.semaphore_signal(
            barrier, inc=1, device_id=(g, lax.rem(s + i, 4)), device_id_type=MESH
        )
    for to_zh in range(2):
        pl.semaphore_signal(
            barrier, inc=1, device_id=(grp(x, 1 - zl, y), to_zh * 2 + c), device_id_type=MESH
        )
    pl.semaphore_wait(barrier, 20)

    homes = (x_ref, dy_ref)
    for a in range(2):
        for h in range(2):

            @pl.loop(1 - h, 8)
            def _(j, a=a, h=h):
                i = j + 8 * h
                tx, ty = shifted(i, 1)
                remote(
                    homes[a].at[tx, :, ty],
                    rows.at[a, c, pl.ds(zl, 2), zh, i],
                    plane_s.at[a],
                    plane_r.at[a, h],
                    (grp(tx, zl, ty), s),
                ).start()

            if h == 0:
                pltpu.make_async_copy(
                    homes[a].at[x, :, y], rows.at[a, c, pl.ds(zl, 2), zh, 0], plane_r.at[a, 0]
                ).start()
        if a == 0:
            pltpu.make_async_copy(place_ref, places.at[s], local_sem.at[5]).start()
            for i in range(1, 4):
                remote(
                    place_ref,
                    places.at[s],
                    seq_s.at[0, i - 1],
                    seq_r.at[0, i - 1],
                    (g, lax.rem(s + i, 4)),
                ).start()

    z_peers = (
        (grp(x, 1 - zl, y), s),
        (grp(x, 1 - zl, y), (1 - zh) * 2 + c),
        (g, (1 - zh) * 2 + c),
    )

    def slots(h):
        return slice(8 * h, 8 * h + 8)

    def block(a, core, zl_, zh_, h):
        return rows.at[a, core, 2 * zl_, zh_, slots(h)]

    def z_out(a, k, h):
        src = rows.at[a, c, 1, zh, slots(h)] if k < 2 else block(a, c, zl, zh, h)
        return remote(
            src, block(a, c, zl, zh, h), z_s.at[a, k, h], z_r.at[a, k, h], z_peers[k]
        )

    where_from = ((1 - zl, zh), (1 - zl, 1 - zh), (zl, 1 - zh), (zl, zh))

    def core_out(a, k, h):
        ref = block(a, c, *where_from[k], h)
        return remote(
            ref, ref, core_s.at[a, k, h], core_r.at[a, k, h], (g, zh * 2 + 1 - c)
        )

    def spread_plane(a, h):
        wait_for(rows.at[a, c, pl.ds(zl, 2), zh, slots(h)], plane_r.at[a, h])
        for k in range(3):
            z_out(a, k, h).start()
        core_out(a, 3, h).start()

    def forward(a, k, h):
        wait_for(block(a, c, *where_from[k], h), z_r.at[a, k, h])
        core_out(a, k, h).start()

    def from_core(a, k):
        for h in range(2):
            wait_for(block(a, 1 - c, *where_from[k], h), core_r.at[a, k, h])

    for copy in weight_copies:
        copy.wait()
    wt[...] = wsl[...].T
    spread_plane(0, 0)
    spread_plane(0, 1)

    wait_for(places.at[0], local_sem.at[5])
    for i in range(1, 4):
        wait_for(places.at[0], seq_r.at[0, i - 1])

    def slot_of(p):
        apart = ((x - (p >> 7)) & 3) * 4 + ((y - (p >> 4)) & 3)
        return ((p >> 6) & 1) * 256 + apart * 16 + (p & 15)

    @pl.loop(0, 4)
    def _(q):
        slot = slot_of(places[q])
        column = jnp.broadcast_to(slot.astype(F32), (128, 512)).T
        lane = lax.broadcasted_iota(jnp.int32, (512, 128), 1).astype(F32)
        for b in range(4):
            perm[q, :, b * 128 : (b + 1) * 128] = jnp.where(
                column == lane + float(b * 128), 1.0, 0.0
            ).astype(BF)

    def ordered(a, q):
        low = rows[a, lax.rem(q, 2), 0, q // 2].reshape(256, 512)
        high = rows[a, lax.rem(q, 2), 2, q // 2].reshape(256, 512)
        return (mm(perm[q, :, :256], low) + mm(perm[q, :, 256:], high)).astype(BF)

    def project(q):
        x_all[q] = ordered(0, q)
        for b in range(4):
            pre = mm(wt[b * 128 : (b + 1) * 128, :], x_all[q], NT)
            sig = 0.5 * jnp.tanh(0.5 * pre) + 0.5
            full = pre * sig
            slope[q, b * 128 : (b + 1) * 128, :] = sig + full * (1.0 - sig)
            cut = full.astype(BF)
            act[q, b * 128 : (b + 1) * 128, :] = cut
            if b == 1:
                vn[q] = cut.T
            if b == 2:
                qn[q] = (cut * BF(0.125)).T
                scaled = cut * BF(0.0625)
                zero = jnp.zeros((64, 512), BF)
                qm[q, 0] = jnp.concatenate([scaled[:64], zero], axis=0)
                qm[q, 1] = jnp.concatenate([zero, scaled[64:]], axis=0)
            if b == 3:
                kn[q] = cut.T

    is_a = seg_ref[0, 0] == seg_ref[0, 1535]
    in_a = jnp.where(is_a, 1.0, 0.0).astype(F32)
    in_b = 1.0 - in_a
    long, short = 1.0 / 1536.0, 1.0 / 512.0
    inv_len = (
        in_a * long + in_b * short, long, long, in_a * short + in_b * long
    )

    def query_of(f):
        return jnp.where(f == 2, 2, jnp.where(is_a, f + 1, 3))

    def key_of(f):
        return jnp.where(f == 2, 1, jnp.where(is_a, 0, 2 - f))

    def causal(rows_, cols):
        return lax.broadcasted_iota(jnp.int32, (rows_, cols), 0) <= lax.broadcasted_iota(
            jnp.int32, (rows_, cols), 1
        )

    def weigh(u, qi, ki, head, half, first, masked):
        keys = pl.ds(half * 256, 256)
        h = mm(kn[ki, keys, :], qm[qi, head, :, first:])
        t = jnp.tanh(h)
        a = 1.0 + t
        w = h * a
        f = a * (1.0 - w) + (w + w)
        if masked:
            keep = causal(256, 512 - first)
            w = jnp.where(keep, w, 0.0)
            f = jnp.where(keep, f, 0.0)
        w = w.astype(BF)
        wc[u, head, keys, first:] = w
        fc[u, head, keys, first:] = f.astype(BF)
        return mm(act[ki, 128 + head * 64 : 192 + head * 64, keys], w)

    def diagonal(q):
        for head in range(2):
            lanes = slice(head * 64, head * 64 + 64)
            out_u[q, lanes, :] = weigh(q, q, q, head, 0, 0, True)
            out_u[q, lanes, 256:] += weigh(q, q, q, head, 1, 256, True)

    forward(0, 0, 0)
    forward(0, 0, 1)
    spread_plane(1, 0)
    forward(0, 1, 0)
    forward(0, 2, 0)
    spread_plane(1, 1)
    from_core(0, 3)
    from_core(0, 0)

    @pl.loop(0, 2)
    def _(j):
        project(zh * 2 + j)

    forward(0, 1, 1)
    forward(0, 2, 1)

    @pl.loop(0, 2)
    def _(j):
        diagonal(zh * 2 + j)

    from_core(0, 1)
    from_core(0, 2)

    @pl.loop(0, 2)
    def _(j):
        project((1 - zh) * 2 + j)

    forward(1, 0, 0)
    forward(1, 0, 1)

    @pl.loop(0, 2)
    def _(j):
        diagonal((1 - zh) * 2 + j)

    @pl.loop(0, 3)
    def _(f):
        qi, ki = query_of(f), key_of(f)
        for head in range(2):
            lanes = slice(head * 64, head * 64 + 64)
            out_u[4 + f, lanes, :] = weigh(4 + f, qi, ki, head, 0, 0, False) + weigh(
                4 + f, qi, ki, head, 1, 0, False
            )

    def mix_back(q):
        dy_all[q] = ordered(1, q)
        dm_t[q] = mm(wo[...], dy_all[q], NT)

    from_core(1, 3)
    from_core(1, 0)

    @pl.loop(0, 2)
    def _(j):
        mix_back(zh * 2 + j)

    for h in range(2):
        forward(1, 1, h)
        forward(1, 2, h)
    from_core(1, 1)
    from_core(1, 2)

    @pl.loop(0, 2)
    def _(j):
        mix_back((1 - zh) * 2 + j)

    for q in range(4):
        total = out_u[q]
        if q == 1:
            total = total + in_a * out_u[4]
        if q == 2:
            total = total + out_u[6] + in_a * out_u[5]
        if q == 3:
            total = total + in_b * (out_u[4] + out_u[5])
        total = total * inv_len[q]
        out_u[q] = total
        centre = jnp.mean(total, axis=0, keepdims=True)
        away = total - centre
        d_normed = dm_t[q] * act[q, :128, :].astype(F32)
        stats[s, 0, q : q + 1, :] = centre
        stats[s, 1, q : q + 1, :] = jnp.sum(away * away, axis=0, keepdims=True)
        stats[s, 2, q : q + 1, :] = jnp.sum(d_normed, axis=0, keepdims=True)
        stats[s, 3, q : q + 1, :] = jnp.sum(d_normed * away, axis=0, keepdims=True)

    def stats_out(i):
        return remote(
            stats.at[s], stats.at[s], seq_s.at[1, i - 1], seq_r.at[1, i - 1],
            (g, lax.rem(s + i, 4)),
        )

    for i in range(1, 4):
        stats_out(i).start()
    for i in range(1, 4):
        wait_for(stats.at[lax.rem(s + i, 4)], seq_r.at[1, 3 - i])

    centres = [stats[r, 0] for r in range(4)]
    mean_all = (centres[0] + centres[1] + centres[2] + centres[3]) * 0.25
    square = jnp.zeros_like(mean_all)
    plain = jnp.zeros_like(mean_all)
    cross = jnp.zeros_like(mean_all)
    for r in range(4):
        off = centres[r] - mean_all
        square += stats[r, 1] + 128.0 * off * off
        plain += stats[r, 2]
        cross += stats[r, 3] + off * stats[r, 2]
    spread_all = lax.rsqrt(square * (1.0 / 512.0) + 1e-5)
    plain = plain * (1.0 / 512.0)
    cross = cross * spread_all * (1.0 / 512.0)

    grad_out = jnp.zeros((128, 512), F32)
    grad_u = jnp.zeros((128, 512), F32)
    for q in range(4):
        gate = act[q, :128, :].astype(F32)
        spread = spread_all[q : q + 1]
        normed = (out_u[q] - mean_all[q : q + 1]) * spread
        d_mixed = dm_t[q]
        mixed = (normed * gate).astype(BF)
        d_u = (d_mixed * normed * slope[q, :128, :]).astype(BF)
        dpre[q, :128, :] = d_u
        d_out = (
            (d_mixed * gate - plain[q : q + 1] - normed * cross[q : q + 1])
            * (spread * (0.5 * inv_len[q]))
        ).astype(BF)
        zero = jnp.zeros((64, 512), BF)
        dom[q, 0] = jnp.concatenate([d_out[:64], zero], axis=0)
        dom[q, 1] = jnp.concatenate([zero, d_out[64:]], axis=0)
        don[q] = d_out.T
        grad_out += mm(mixed, dy_all[q])
        grad_u += mm(d_u, x_all[q])

    def grads_out(buf, got, sem):
        @pl.loop(1, 16)
        def _(i):
            tx, ty = shifted(i, 1)
            remote(
                buf.at[tx, :, ty], got.at[i], sem.at[0], sem.at[1], (grp(tx, zl, ty), s)
            ).start()

        pltpu.make_async_copy(buf.at[x, :, y], got.at[0], sem.at[1]).start()

    ge_s[:, :, :, 0] = grad_u.T.astype(BF).reshape(4, 2, 4, 16, 128)
    for b in range(4):
        ge_s[b, :, :, 1] = (
            grad_out[:, b * 128 : (b + 1) * 128].astype(BF).reshape(2, 4, 16, 128)
        )
    grads_out(ge_s, ge_r, ge_sem)

    first = jnp.where(c == 0, x, y)
    second = jnp.where(c == 0, y, x)
    zz = zl * 2 + zh
    reduced = ((ge_r, ge_sem), (gl_r, gl_sem))
    met = (met_e, met_l)
    summed = (mine_e, mine_l)
    gathered = (age, agl)

    def z_copies(t):
        ref = met[t].at[zz]
        return [
            remote(ref, ref, ag_s.at[t, 0, k], ag_r.at[t, 0, k], peer)
            for k, peer in enumerate(z_peers)
        ]

    def meet(t):
        got, sem = reduced[t]
        wait_for(got, sem.at[1])
        met[t][zz] = jnp.sum(got[...].astype(F32), axis=0)
        for copy in z_copies(t):
            copy.start()

    def along(i, on_first):
        nf = lax.rem(first + i, 4) if on_first else first
        ns = second if on_first else lax.rem(second + i, 4)
        nx = jnp.where(c == 0, nf, ns)
        ny = jnp.where(c == 0, ns, nf)
        return (grp(nx, zl, ny), s)

    def own_copy(t):
        return pltpu.make_async_copy(
            summed[t], gathered[t].at[c, first, second], ag_l.at[t]
        )

    def second_copies(t):
        return [
            remote(
                summed[t], gathered[t].at[c, first, second],
                ag_s.at[t, 1, i - 1], ag_r.at[t, 1, i - 1], along(i, False),
            )
            for i in range(1, 4)
        ]

    def first_copies(t):
        ref = gathered[t].at[c, first]
        return [
            remote(ref, ref, ag_s.at[t, 2, i - 1], ag_r.at[t, 2, i - 1], along(i, True))
            for i in range(1, 4)
        ]

    def came(i):
        return lax.rem(first + 4 - i, 4)

    def core_copy(t, i):
        ref = gathered[t].at[c, came(i)]
        return remote(
            ref, ref, ag_s.at[t, 3, i], ag_r.at[t, 3, i], (g, zh * 2 + 1 - c)
        )

    def gather_second(t):
        for k in range(3):
            wait_for(met[t].at[0], ag_r.at[t, 0, k])
        for chunk in range(2):
            for to_zh in range(2):
                summed[t][chunk * 2 + to_zh] = (
                    met[t][to_zh, chunk] + met[t][2 + to_zh, chunk]
                ).astype(BF)
        own_copy(t).start()
        for copy in second_copies(t):
            copy.start()

    def gather_first(t):
        own_copy(t).wait()
        for i in range(1, 4):
            wait_for(gathered[t].at[c, first, second], ag_r.at[t, 1, i - 1])
        for copy in first_copies(t):
            copy.start()
        core_copy(t, 0).start()

    def gather_core(t):
        for i in range(1, 4):
            wait_for(gathered[t].at[c, came(i)], ag_r.at[t, 2, i - 1])
            core_copy(t, i).start()

    def gather_end(t):
        for i in range(4):
            wait_for(gathered[t].at[1 - c, 0], ag_r.at[t, 3, i])

    def attend_back(u, qi, ki, masked):
        lane = lax.broadcasted_iota(jnp.int32, (256, 128), 1)
        for half in range(2):
            keys = pl.ds(half * 256, 256)
            first_q = 256 if masked and half == 1 else 0
            d_v, d_k = [], []
            for head in range(2):
                d_w = mm(vn[ki, keys, :], dom[qi, head, :, first_q:])
                d_s = (d_w * fc[u, head, keys, first_q:].astype(F32)).astype(BF)
                d_v.append(mm(wc[u, head, keys, first_q:], don[qi, first_q:, :]))
                d_k.append(mm(d_s, qn[qi, first_q:, :]))
                part = mm(act[ki, 384 + head * 64 : 448 + head * 64, keys], d_s)
                lanes = slice(head * 64, head * 64 + 64)
                if half == 0:
                    out_u[u, lanes, :] = part
                else:
                    out_u[u, lanes, first_q:] += part
            dv_u[u, keys, :] = jnp.where(lane < 64, d_v[0], d_v[1])
            dk_u[u, keys, :] = jnp.where(lane < 64, d_k[0], d_k[1])

    def finish(q):
        d_q, d_k, d_v = out_u[q], dk_u[q], dv_u[q]
        if q == 0:
            d_k = d_k + in_a * (dk_u[4] + dk_u[5])
            d_v = d_v + in_a * (dv_u[4] + dv_u[5])
        if q == 1:
            d_q = d_q + in_a * out_u[4]
            d_k = d_k + dk_u[6] + in_b * dk_u[5]
            d_v = d_v + dv_u[6] + in_b * dv_u[5]
        if q == 2:
            d_q = d_q + out_u[6] + in_a * out_u[5]
            d_k = d_k + in_b * dk_u[4]
            d_v = d_v + in_b * dv_u[4]
        if q == 3:
            d_q = d_q + in_b * (out_u[4] + out_u[5])
        dpre[q, 128:256, :] = (2.0 * d_v.T * slope[q, 128:256, :]).astype(BF)
        dpre[q, 256:384, :] = (0.125 * d_q * slope[q, 256:384, :]).astype(BF)
        dpre[q, 384:512, :] = (d_k.T * slope[q, 384:512, :]).astype(BF)

    def dx_core(k):
        return remote(
            dxs.at[k], dxp.at[k], dxc_s.at[k], dxc_r.at[k], (g, zh * 2 + 1 - c)
        )

    def to_partner(k):
        q = 3 * (1 - c) if k == 0 else 1 + c
        dxs[k] = mm(dpre[q], wt[...], TN).astype(BF)
        dx_core(k).start()

    def rows_of(zl_, h):
        return pl.ds(pl.multiple_of(zl_ * 256 + h * 128, 128), 128)

    def dx_across(k, h):
        to_zh = c if k == 0 else 1 - c
        code = jnp.where(to_zh == zh, 0, 1)
        return remote(
            dxs.at[2 + k, rows_of(1 - zl, h)], zr.at[code, h],
            dxz_s.at[code, h], dxz_r.at[code, h],
            (grp(x, 1 - zl, y), to_zh * 2 + c),
        )

    def dx_same(k, h):
        return remote(
            dxs.at[2 + k, rows_of(zl, h)], zr.at[2, h], dxz_s.at[2, h], dxz_r.at[2, h],
            (g, (1 - zh) * 2 + c),
        )

    def to_planes(k):
        q = 3 * c if k == 0 else 2 - c
        to_zh = c if k == 0 else 1 - c
        mine = mm(dpre[q], wt[...], TN)
        wait_for(dxp.at[k], dxc_r.at[k])
        both = (mine + dxp[k].astype(F32)).astype(BF)
        back = jnp.where(
            lax.broadcasted_iota(jnp.int32, (512, 512), 0) == slot_of(places[q]), 1.0, 0.0
        ).astype(BF)
        dxs[2 + k] = mm(back, both).astype(BF)

        for h in range(2):

            @pl.when(to_zh != zh)
            def _(h=h):
                dx_same(k, h).start()

            dx_across(k, h).start()

    @pl.loop(0, 2)
    def _(f):
        attend_back(4 + f, query_of(f), key_of(f), False)

    @pl.loop(0, 2)
    def _(i):
        attend_back(3 * i, 3 * i, 3 * i, True)

    finish(0)
    finish(3)
    to_partner(0)
    meet(0)
    for q in (0, 3):
        part = mm(dpre[q, 128:, :], x_all[q])
        if q == 0:
            acc[...] = part
        else:
            acc[...] += part
    to_planes(0)

    @pl.loop(1, 3)
    def _(q):
        attend_back(q, q, q, True)

    gather_second(0)
    attend_back(6, 2, 1, False)
    finish(1)
    finish(2)
    to_partner(1)
    total = acc[...] + mm(dpre[1, 128:, :], x_all[1]) + mm(dpre[2, 128:, :], x_all[2])
    for b in range(3):
        gl_s[:, :, :, b] = (
            total[b * 128 : (b + 1) * 128].T.astype(BF).reshape(4, 2, 4, 16, 128)
        )
    grads_out(gl_s, gl_r, gl_sem)
    to_planes(1)

    def go_home(h):
        for k in range(3):
            wait_for(zr.at[k, h], dxz_r.at[k, h])
        keep = jnp.where(c == zh, 2, 3)
        own = (dxs[keep, rows_of(zl, h)].astype(F32) + zr[2, h].astype(F32)).astype(BF)
        other = (zr[0, h].astype(F32) + zr[1, h].astype(F32)).astype(BF)
        fin[pl.ds(zl, 1), slots(h)] = own.reshape(1, 8, 16, 512)
        fin[pl.ds(1 - zl, 1), slots(h)] = other.reshape(1, 8, 16, 512)

        @pl.loop(1 - h, 8)
        def _(j):
            i = j + 8 * h
            tx, ty = shifted(i, -1)
            remote(
                fin.at[:, i], dx_out.at[x, :, y], home_sem.at[0], home_sem.at[1],
                (grp(tx, zl, ty), s),
            ).start()

        if h == 0:
            pltpu.make_async_copy(fin.at[:, 0], dx_out.at[x, :, y], home_sem.at[1]).start()

    meet(1)
    gather_first(0)
    gather_second(1)
    go_home(0)
    gather_first(1)
    go_home(1)
    gather_core(0)
    gather_core(1)
    gather_end(0)
    gather_end(1)

    wait_for(dx_out, home_sem.at[1])
    wait_for(fin.at[:, 0:15], home_sem.at[0])
    for t in range(2):
        for copy in z_copies(t) + second_copies(t) + first_copies(t):
            copy.wait_send()
        for i in range(4):
            core_copy(t, i).wait_send()
    for a in range(2):
        wait_for(rows.at[a, c, 0:2, 0, 0:15], plane_s.at[a])
        for h in range(2):
            for k in range(3):
                z_out(a, k, h).wait_send()
            for k in range(4):
                core_out(a, k, h).wait_send()
    for i in range(1, 4):
        wait_for(places.at[0], seq_s.at[0, i - 1])
        stats_out(i).wait_send()
    for k in range(2):
        dx_core(k).wait_send()
    for h in range(2):
        for k in range(3):
            wait_for(zr.at[k, h], dxz_s.at[k, h])
    wait_for(ge_r.at[0:15], ge_sem.at[0])
    wait_for(gl_r.at[0:15], gl_sem.at[0])


def finish_kernel(dx_ref, dy_ref, e0, e1, l0, l1, dx_out, gin_out, gout_out):
    factor = 1.0 / 256.0
    dx_out[...] = (dx_ref[...].astype(F32) + dy_ref[...].astype(F32)).astype(BF)
    for core in range(2):
        for y in range(4):
            for z in range(4):
                zl, position = z // 2, (z % 2) * 2 + core
                early = e0[0, 0, y, z] if core == 0 else e1[0, y, 0, z]
                late = l0[0, 0, y, z] if core == 0 else l1[0, y, 0, z]
                at = slice((zl * 4 + y) * 16, (zl * 4 + y) * 16 + 16)
                for b in range(4):
                    lo = b * 512 + position * 128
                    part = early[0] if b == 0 else late[b - 1]
                    gin_out[at, lo : lo + 128] = part.astype(F32) * factor
                lo = position * 128 + (zl * 4 + y) * 16
                gout_out[lo : lo + 16, :] = early[1].astype(F32) * factor


def per_device(x_home, dy_home, w_in, w_out, place, seg_ids):
    shape = (4, 2, 4, 16, 512)
    vm = pltpu.VMEM
    dma = pltpu.SemaphoreType.DMA
    hbm = pl.BlockSpec(memory_space=pl.ANY)
    in_vmem = pl.BlockSpec(memory_space=pltpu.VMEM)
    dx, early, late = pl.pallas_call(
        kernel,
        out_shape=(
            jax.ShapeDtypeStruct(shape, BF),
            jax.ShapeDtypeStruct((2, 4, 4, 4, 2, 16, 128), BF),
            jax.ShapeDtypeStruct((2, 4, 4, 4, 3, 16, 128), BF),
        ),
        in_specs=[
            hbm, hbm, hbm, hbm, in_vmem, pl.BlockSpec(memory_space=pltpu.SMEM),
        ],
        out_specs=(hbm, hbm, hbm),
        scratch_shapes=[
            vm((2, 2, 3, 2, 16, 16, 512), BF),
            vm((4, 512, 512), BF),
            vm((4, 512, 512), BF),
            vm((4, 512, 512), BF),
            vm((4, 512, 512), BF),
            vm((4, 512, 512), F32),
            vm((4, 2, 128, 512), BF),
            vm((4, 512, 128), BF),
            vm((4, 512, 128), BF),
            vm((4, 512, 128), BF),
            vm((7, 2, 512, 512), BF),
            vm((7, 2, 512, 512), BF),
            vm((7, 128, 512), F32),
            vm((4, 128, 512), F32),
            vm((4, 4, 4, 512), F32),
            vm((4, 2, 128, 512), BF),
            vm((4, 512, 128), BF),
            vm((7, 512, 128), F32),
            vm((7, 512, 128), F32),
            vm((4, 512, 512), BF),
            vm((512, 512), BF),
            vm((512, 512), BF),
            vm((128, 512), BF),
            vm((4, 1, 512), jnp.int32),
            vm((4, 2, 4, 2, 16, 128), BF),
            vm((16, 2, 2, 16, 128), BF),
            vm((4, 2, 4, 3, 16, 128), BF),
            vm((16, 2, 3, 16, 128), BF),
            vm((4, 2, 2, 16, 128), F32),
            vm((4, 2, 16, 128), BF),
            vm((4, 2, 3, 16, 128), F32),
            vm((4, 3, 16, 128), BF),
            vm((384, 512), F32),
            vm((4, 512, 512), BF),
            vm((2, 512, 512), BF),
            vm((3, 2, 128, 512), BF),
            vm((2, 16, 16, 512), BF),
            dma((6,)), dma((2,)), dma((2, 2)), dma((2, 3, 2)), dma((2, 3, 2)),
            dma((2, 4, 2)), dma((2, 4, 2)), dma((2, 3)), dma((2, 3)), dma((2,)), dma((2,)),
            dma((2, 4, 4)), dma((2, 4, 4)), dma((2,)), dma((2,)), dma((2,)),
            dma((3, 2)), dma((3, 2)), dma((2,)),
        ],
        compiler_params=pltpu.CompilerParams(
            collective_id=0, has_side_effects=True, vmem_limit_bytes=63 * 2**20
        ),
    )(
        x_home.reshape(shape),
        dy_home.reshape(shape),
        w_in,
        w_out,
        place.reshape(1, 512),
        seg_ids.reshape(1, 2048),
    )
    row = pl.BlockSpec((128, 512), lambda i: (i, 0))

    def part(core, blocks):
        if core == 0:
            return pl.BlockSpec((1, 1, 4, 4, blocks, 16, 128), lambda i: (0, i, 0, 0, 0, 0, 0))
        return pl.BlockSpec((1, 4, 1, 4, blocks, 16, 128), lambda i: (1, 0, i, 0, 0, 0, 0))

    return pl.pallas_call(
        finish_kernel,
        grid=(4,),
        out_shape=(
            jax.ShapeDtypeStruct((512, 512), BF),
            jax.ShapeDtypeStruct((512, 2048), F32),
            jax.ShapeDtypeStruct((512, 512), F32),
        ),
        in_specs=[row, row, part(0, 2), part(1, 2), part(0, 3), part(1, 3)],
        out_specs=(
            row,
            pl.BlockSpec((128, 2048), lambda i: (i, 0)),
            pl.BlockSpec((512, 128), lambda i: (0, i)),
        ),
    )(dx.reshape(512, 512), dy_home, early, early, late, late)


def solution(mesh):
    in_specs = (
        P(("grp", "seq"), None),
        P(("grp", "seq"), None),
        P(),
        P(),
        P("grp", "seq", None),
        P("grp", None),
    )
    out_specs = (P(("grp", "seq"), None), P(), P())
    return jax.shard_map(
        per_device, mesh=mesh, in_specs=in_specs, out_specs=out_specs, check_vma=False
    )
```

time: 125 us -> 105 us (0.84)
  Pallas kernels: 116 us -> 104 us
  local copies, waits for them, and re-layouts: 7.63 us -> 0 us
    pallas_call x1, Pallas kernels: 116 us -> 99.2 us  [per_device(): pl.pallas_call(kernel, out_shape=(jax.ShapeDtypeStruct(shape, BF), jax.Sh...]
    unnamed x5 -> x0, local copies, waits for them, and re-layouts: 7.63 us -> none
    pallas_call x0 -> x1, Pallas kernels: none -> 5.11 us  [per_device(): pl.pallas_call(finish_kernel, grid=(4,), out_shape=(jax.ShapeDtypeStruct(...]
where the time goes in v1:
time: 105 us
  Pallas kernels  104 us (99%)
    pallas_call x1, Pallas kernels, per_device(): pl.pallas_call(kernel, out_shape=(jax.ShapeDtypeStruct(shape, BF), jax.Sh...  99.2 us
    pallas_call x1, Pallas kernels, per_device(): pl.pallas_call(finish_kernel, grid=(4,), out_shape=(jax.ShapeDtypeStruct(...  5.11 us

profile of v1, /device:TPU:1, one launch (start us, length us, event | category | flops | bytes accessed | tf_op | source)
XLA Modules:
  0.0 104.9 jit_solution(18416378451469891739)
XLA Ops:
  0.6 99.2 %shard_map.85 = (bf16[4,2,4,16,512]{4,3,2,1,0:T(8,128)(2,1)}, bf16[2,4,4,4,2,16,128]{6,5,4,3,2,1,0:T(8,128)(2,1)}, bf16[2,4,4,4,3,16,128]{6,5,4,3,2,1,0:T(8,128)(2,1)}) custom-call(bf16[4,2,4,16,512]{4,3,2,1,0:T(8,128)(2,1)} %bitcast.5, bf16[4,2,4,16,512]{4,3,2,1,0:T(8,128)(2,1)} %bitcast.4, bf16[512,2048]{1,0:T(8,128)(2,1)} %win_ref.1, ...), custom_call_target="tpu_custom_call" | custom-call | tf_op jit(solution)/shard_map/pallas_call | solution.py:690
  99.8 5.1 %shard_map.86 = (bf16[512,512]{1,0:T(8,128)(2,1)}, f32[512,2048]{1,0:T(8,128)}, f32[512,512]{1,0:T(8,128)}) custom-call(bf16[512,512]{1,0:T(8,128)(2,1)} %bitcast.6, bf16[512,512]{1,0:T(8,128)(2,1)} %dy_ref.1, bf16[2,4,4,4,2,16,128]{6,5,4,3,2,1,0:T(8,128)(2,1)} %get-tuple-element.7.e0.e1, bf16[2,4,4,4,2,16,128]{6,5,4,3,2,1,0:T(8,128)(2,1)} %get-tuple-element.7.e0.e1, ...), custom_call_target="tpu_custom_call" | custom-call | tf_op jit(solution)/shard_map/pallas_call | solution.py:762

commit v2 on v1

--- a/solution.py
+++ b/solution.py
@@ -35,11 +35,11 @@
 def kernel(
     x_ref, dy_ref, win_ref, wout_ref, place_ref, seg_ref,
     dx_out, age, agl,
-    rows, perm, x_all, dy_all, act, slope, qm, qn, kn, vn, wc, fc, out_u, dm_t, stats,
+    rows, perm, x_all, dy_all, act, slope, qm, qn, kn, vn, wc, fc, out_u, out_t, dm_t, stats,
     dom, don, dv_u, dk_u, dpre, wsl, wt, wo, places,
     ge_s, ge_r, gl_s, gl_r, met_e, mine_e, met_l, mine_l, acc, dxs, dxp, zr, fin,
     local_sem, plane_s, plane_r, z_s, z_r, core_s, core_r, seq_s, seq_r, ge_sem, gl_sem,
-    ag_s, ag_r, ag_l, dxc_s, dxc_r, dxz_s, dxz_r, home_sem,
+    ag_s, ag_r, ag_l, first_r, other_r, dxc_s, dxc_r, dxz_s, dxz_r, home_sem,
 ):
     g = lax.axis_index("grp")
     s = lax.axis_index("seq")
@@ -114,7 +114,7 @@
                 remote(
                     place_ref,
                     places.at[s],
-                    seq_s.at[0, i - 1],
+                    seq_s.at[0],
                     seq_r.at[0, i - 1],
                     (g, lax.rem(s + i, 4)),
                 ).start()
@@ -134,7 +134,7 @@
     def z_out(a, k, h):
         src = rows.at[a, c, 1, zh, slots(h)] if k < 2 else block(a, c, zl, zh, h)
         return remote(
-            src, block(a, c, zl, zh, h), z_s.at[a, k, h], z_r.at[a, k, h], z_peers[k]
+            src, block(a, c, zl, zh, h), z_s.at[a], z_r.at[a, k, h], z_peers[k]
         )
 
     where_from = ((1 - zl, zh), (1 - zl, 1 - zh), (zl, 1 - zh), (zl, zh))
@@ -142,7 +142,7 @@
     def core_out(a, k, h):
         ref = block(a, c, *where_from[k], h)
         return remote(
-            ref, ref, core_s.at[a, k, h], core_r.at[a, k, h], (g, zh * 2 + 1 - c)
+            ref, ref, core_s.at[a], core_r.at[a, k, h], (g, zh * 2 + 1 - c)
         )
 
     def spread_plane(a, h):
@@ -283,8 +283,7 @@
     def _(j):
         diagonal((1 - zh) * 2 + j)
 
-    @pl.loop(0, 3)
-    def _(f):
+    def across(f):
         qi, ki = query_of(f), key_of(f)
         for head in range(2):
             lanes = slice(head * 64, head * 64 + 64)
@@ -292,48 +291,51 @@
                 4 + f, qi, ki, head, 1, 0, False
             )
 
-    def mix_back(q):
+    @pl.loop(0, 2)
+    def _(f):
+        across(f)
+
+    for k in (1, 2):
+        forward(1, k, 0)
+    across(2)
+
+    def sums(q):
         dy_all[q] = ordered(1, q)
-        dm_t[q] = mm(wo[...], dy_all[q], NT)
+        d_mixed = mm(wo[...], dy_all[q], NT)
+        dm_t[q] = d_mixed
+        with_4 = jnp.where(q == 1, in_a, jnp.where(q == 3, in_b, 0.0))
+        with_5 = jnp.where(q == 2, in_a, jnp.where(q == 3, in_b, 0.0))
+        with_6 = jnp.where(q == 2, 1.0, 0.0)
+        total = out_u[q] + with_4 * out_u[4] + with_5 * out_u[5] + with_6 * out_u[6]
+        total = total * jnp.where(q == 0, inv_len[0], jnp.where(q == 3, inv_len[3], long))
+        out_t[q] = total
+        centre = jnp.mean(total, axis=0, keepdims=True)
+        away = total - centre
+        d_normed = d_mixed * act[q, :128, :].astype(F32)
+        stats[s, q, 0:1, :] = centre
+        stats[s, q, 1:2, :] = jnp.sum(away * away, axis=0, keepdims=True)
+        stats[s, q, 2:3, :] = jnp.sum(d_normed, axis=0, keepdims=True)
+        stats[s, q, 3:4, :] = jnp.sum(d_normed * away, axis=0, keepdims=True)
 
     from_core(1, 3)
     from_core(1, 0)
 
     @pl.loop(0, 2)
     def _(j):
-        mix_back(zh * 2 + j)
-
-    for h in range(2):
-        forward(1, 1, h)
-        forward(1, 2, h)
+        sums(zh * 2 + j)
+
+    for k in (1, 2):
+        forward(1, k, 1)
     from_core(1, 1)
     from_core(1, 2)
 
     @pl.loop(0, 2)
     def _(j):
-        mix_back((1 - zh) * 2 + j)
-
-    for q in range(4):
-        total = out_u[q]
-        if q == 1:
-            total = total + in_a * out_u[4]
-        if q == 2:
-            total = total + out_u[6] + in_a * out_u[5]
-        if q == 3:
-            total = total + in_b * (out_u[4] + out_u[5])
-        total = total * inv_len[q]
-        out_u[q] = total
-        centre = jnp.mean(total, axis=0, keepdims=True)
-        away = total - centre
-        d_normed = dm_t[q] * act[q, :128, :].astype(F32)
-        stats[s, 0, q : q + 1, :] = centre
-        stats[s, 1, q : q + 1, :] = jnp.sum(away * away, axis=0, keepdims=True)
-        stats[s, 2, q : q + 1, :] = jnp.sum(d_normed, axis=0, keepdims=True)
-        stats[s, 3, q : q + 1, :] = jnp.sum(d_normed * away, axis=0, keepdims=True)
+        sums((1 - zh) * 2 + j)
 
     def stats_out(i):
         return remote(
-            stats.at[s], stats.at[s], seq_s.at[1, i - 1], seq_r.at[1, i - 1],
+            stats.at[s], stats.at[s], seq_s.at[1], seq_r.at[1, i - 1],
             (g, lax.rem(s + i, 4)),
         )
 
@@ -342,16 +344,16 @@
     for i in range(1, 4):
         wait_for(stats.at[lax.rem(s + i, 4)], seq_r.at[1, 3 - i])
 
-    centres = [stats[r, 0] for r in range(4)]
+    centres = [stats[r, :, 0, :] for r in range(4)]
     mean_all = (centres[0] + centres[1] + centres[2] + centres[3]) * 0.25
     square = jnp.zeros_like(mean_all)
     plain = jnp.zeros_like(mean_all)
     cross = jnp.zeros_like(mean_all)
     for r in range(4):
         off = centres[r] - mean_all
-        square += stats[r, 1] + 128.0 * off * off
-        plain += stats[r, 2]
-        cross += stats[r, 3] + off * stats[r, 2]
+        square += stats[r, :, 1, :] + 128.0 * off * off
+        plain += stats[r, :, 2, :]
+        cross += stats[r, :, 3, :] + off * stats[r, :, 2, :]
     spread_all = lax.rsqrt(square * (1.0 / 512.0) + 1e-5)
     plain = plain * (1.0 / 512.0)
     cross = cross * spread_all * (1.0 / 512.0)
@@ -361,7 +363,7 @@
     for q in range(4):
         gate = act[q, :128, :].astype(F32)
         spread = spread_all[q : q + 1]
-        normed = (out_u[q] - mean_all[q : q + 1]) * spread
+        normed = (out_t[q] - mean_all[q : q + 1]) * spread
         d_mixed = dm_t[q]
         mixed = (normed * gate).astype(BF)
         d_u = (d_mixed * normed * slope[q, :128, :]).astype(BF)
@@ -405,7 +407,7 @@
     def z_copies(t):
         ref = met[t].at[zz]
         return [
-            remote(ref, ref, ag_s.at[t, 0, k], ag_r.at[t, 0, k], peer)
+            remote(ref, ref, ag_s.at[t, 0], ag_r.at[t, 0, k], peer)
             for k, peer in enumerate(z_peers)
         ]
 
@@ -423,37 +425,42 @@
         ny = jnp.where(c == 0, ns, nf)
         return (grp(nx, zl, ny), s)
 
+    def piece(t, i, j):
+        return gathered[t].at[
+            c, lax.rem(first + 4 - j, 4), lax.rem(second + 4 - i, 4)
+        ]
+
+    def held(t, i):
+        return summed[t] if i == 0 else piece(t, i, 0)
+
     def own_copy(t):
-        return pltpu.make_async_copy(
-            summed[t], gathered[t].at[c, first, second], ag_l.at[t]
-        )
+        return pltpu.make_async_copy(summed[t], piece(t, 0, 0), ag_l.at[t])
 
     def second_copies(t):
         return [
             remote(
-                summed[t], gathered[t].at[c, first, second],
-                ag_s.at[t, 1, i - 1], ag_r.at[t, 1, i - 1], along(i, False),
+                summed[t], piece(t, 0, 0),
+                ag_s.at[t, 1], ag_r.at[t, 1, i - 1], along(i, False),
             )
             for i in range(1, 4)
         ]
 
-    def first_copies(t):
-        ref = gathered[t].at[c, first]
+    def first_copies(t, i):
         return [
-            remote(ref, ref, ag_s.at[t, 2, i - 1], ag_r.at[t, 2, i - 1], along(i, True))
-            for i in range(1, 4)
+            remote(
+                held(t, i), piece(t, i, 0),
+                ag_s.at[t, 2], first_r.at[t, i, j - 1], along(j, True),
+            )
+            for j in range(1, 4)
         ]
 
-    def came(i):
-        return lax.rem(first + 4 - i, 4)
-
-    def core_copy(t, i):
-        ref = gathered[t].at[c, came(i)]
+    def core_copy(t, i, j):
         return remote(
-            ref, ref, ag_s.at[t, 3, i], ag_r.at[t, 3, i], (g, zh * 2 + 1 - c)
-        )
-
-    def gather_second(t):
+            held(t, i) if j == 0 else piece(t, i, j), piece(t, i, j),
+            ag_s.at[t, 3], other_r.at[t], (g, zh * 2 + 1 - c),
+        )
+
+    def gather_start(t):
         for k in range(3):
             wait_for(met[t].at[0], ag_r.at[t, 0, k])
         for chunk in range(2):
@@ -461,26 +468,27 @@
                 summed[t][chunk * 2 + to_zh] = (
                     met[t][to_zh, chunk] + met[t][2 + to_zh, chunk]
                 ).astype(BF)
+        for copy in second_copies(t) + first_copies(t, 0):
+            copy.start()
+        core_copy(t, 0, 0).start()
         own_copy(t).start()
-        for copy in second_copies(t):
-            copy.start()
-
-    def gather_first(t):
+
+    def gather_pass(t):
+        for i in range(1, 4):
+            wait_for(piece(t, i, 0), ag_r.at[t, 1, i - 1])
+            for copy in first_copies(t, i):
+                copy.start()
+            core_copy(t, i, 0).start()
+
+    def gather_core(t):
+        for i in range(4):
+            for j in range(1, 4):
+                wait_for(piece(t, i, j), first_r.at[t, i, j - 1])
+                core_copy(t, i, j).start()
+
+    def gather_end(t):
         own_copy(t).wait()
-        for i in range(1, 4):
-            wait_for(gathered[t].at[c, first, second], ag_r.at[t, 1, i - 1])
-        for copy in first_copies(t):
-            copy.start()
-        core_copy(t, 0).start()
-
-    def gather_core(t):
-        for i in range(1, 4):
-            wait_for(gathered[t].at[c, came(i)], ag_r.at[t, 2, i - 1])
-            core_copy(t, i).start()
-
-    def gather_end(t):
-        for i in range(4):
-            wait_for(gathered[t].at[1 - c, 0], ag_r.at[t, 3, i])
+        wait_for(gathered[t].at[1 - c], other_r.at[t])
 
     def attend_back(u, qi, ki, masked):
         lane = lax.broadcasted_iota(jnp.int32, (256, 128), 1)
@@ -523,7 +531,7 @@
 
     def dx_core(k):
         return remote(
-            dxs.at[k], dxp.at[k], dxc_s.at[k], dxc_r.at[k], (g, zh * 2 + 1 - c)
+            dxs.at[k], dxp.at[k], dxc_s.at[0], dxc_r.at[k], (g, zh * 2 + 1 - c)
         )
 
     def to_partner(k):
@@ -539,13 +547,13 @@
         code = jnp.where(to_zh == zh, 0, 1)
         return remote(
             dxs.at[2 + k, rows_of(1 - zl, h)], zr.at[code, h],
-            dxz_s.at[code, h], dxz_r.at[code, h],
+            dxz_s.at[0], dxz_r.at[code, h],
             (grp(x, 1 - zl, y), to_zh * 2 + c),
         )
 
     def dx_same(k, h):
         return remote(
-            dxs.at[2 + k, rows_of(zl, h)], zr.at[2, h], dxz_s.at[2, h], dxz_r.at[2, h],
+            dxs.at[2 + k, rows_of(zl, h)], zr.at[2, h], dxz_s.at[0], dxz_r.at[2, h],
             (g, (1 - zh) * 2 + c),
         )
 
@@ -592,7 +600,7 @@
     def _(q):
         attend_back(q, q, q, True)
 
-    gather_second(0)
+    gather_start(0)
     attend_back(6, 2, 1, False)
     finish(1)
     finish(2)
@@ -626,11 +634,20 @@
         if h == 0:
             pltpu.make_async_copy(fin.at[:, 0], dx_out.at[x, :, y], home_sem.at[1]).start()
 
+    for a in range(2):
+        wait_for(rows.at[a, c, 0:2, 0, 0:15], plane_s.at[a])
+        wait_for(rows.at[a, c, :, 0], z_s.at[a])
+        wait_for(rows.at[a, c, 0:2], core_s.at[a])
+    wait_for(places.at[0:3], seq_s.at[0])
+    wait_for(stats.at[0:3], seq_s.at[1])
+    wait_for(dxs.at[0:2], dxc_s.at[0])
+    wait_for(ge_r.at[0:15], ge_sem.at[0])
     meet(1)
-    gather_first(0)
-    gather_second(1)
+    wait_for(gl_r.at[0:15], gl_sem.at[0])
+    gather_pass(0)
+    gather_start(1)
+    gather_pass(1)
     go_home(0)
-    gather_first(1)
     go_home(1)
     gather_core(0)
     gather_core(1)
@@ -639,46 +656,72 @@
 
     wait_for(dx_out, home_sem.at[1])
     wait_for(fin.at[:, 0:15], home_sem.at[0])
+    wait_for(zr, dxz_s.at[0])
     for t in range(2):
-        for copy in z_copies(t) + second_copies(t) + first_copies(t):
-            copy.wait_send()
-        for i in range(4):
-            core_copy(t, i).wait_send()
-    for a in range(2):
-        wait_for(rows.at[a, c, 0:2, 0, 0:15], plane_s.at[a])
-        for h in range(2):
-            for k in range(3):
-                z_out(a, k, h).wait_send()
-            for k in range(4):
-                core_out(a, k, h).wait_send()
-    for i in range(1, 4):
-        wait_for(places.at[0], seq_s.at[0, i - 1])
-        stats_out(i).wait_send()
-    for k in range(2):
-        dx_core(k).wait_send()
-    for h in range(2):
-        for k in range(3):
-            wait_for(zr.at[k, h], dxz_s.at[k, h])
-    wait_for(ge_r.at[0:15], ge_sem.at[0])
-    wait_for(gl_r.at[0:15], gl_sem.at[0])
-
-
-def finish_kernel(dx_ref, dy_ref, e0, e1, l0, l1, dx_out, gin_out, gout_out):
+        wait_for(met[t].at[0:3], ag_s.at[t, 0])
+        wait_for(gathered[t].at[0, 0, 0:3], ag_s.at[t, 1])
+        wait_for(gathered[t].at[0, 0:3], ag_s.at[t, 2])
+        wait_for(gathered[t].at[0], ag_s.at[t, 3])
+
+
+def finish_kernel(dx_ref, dy_ref, e_ref, l_ref, dx_out, gin_out, gout_out, e, l, dxv, dyv, gin, gout, sem, out_sem):
     factor = 1.0 / 256.0
-    dx_out[...] = (dx_ref[...].astype(F32) + dy_ref[...].astype(F32)).astype(BF)
-    for core in range(2):
-        for y in range(4):
-            for z in range(4):
-                zl, position = z // 2, (z % 2) * 2 + core
-                early = e0[0, 0, y, z] if core == 0 else e1[0, y, 0, z]
-                late = l0[0, 0, y, z] if core == 0 else l1[0, y, 0, z]
-                at = slice((zl * 4 + y) * 16, (zl * 4 + y) * 16 + 16)
-                for b in range(4):
-                    lo = b * 512 + position * 128
-                    part = early[0] if b == 0 else late[b - 1]
-                    gin_out[at, lo : lo + 128] = part.astype(F32) * factor
-                lo = position * 128 + (zl * 4 + y) * 16
-                gout_out[lo : lo + 16, :] = early[1].astype(F32) * factor
+    loads = []
+    for core, axis in ((1, 0), (1, 1), (1, 2), (1, 3), (0, 0), (0, 1), (0, 2), (0, 3)):
+        k = len(loads)
+        loads.append(
+            (
+                pltpu.make_async_copy(e_ref.at[core, axis], e.at[core, axis], sem.at[0, k]),
+                pltpu.make_async_copy(l_ref.at[core, axis], l.at[core, axis], sem.at[1, k]),
+            )
+        )
+        for copy in loads[-1]:
+            copy.start()
+    rows_in = (
+        pltpu.make_async_copy(dx_ref, dxv, sem.at[0, 8]),
+        pltpu.make_async_copy(dy_ref, dyv, sem.at[1, 8]),
+    )
+    for copy in rows_in:
+        copy.start()
+    for pair in loads[:4]:
+        for copy in pair:
+            copy.wait()
+    stores = []
+    for x in range(4):
+        for copy in loads[4 + x]:
+            copy.wait()
+        for core in range(2):
+            for y in range(4):
+                for z in range(4):
+                    position = (z % 2) * 2 + core
+                    at = (core, x, y, z) if core == 0 else (core, y, x, z)
+                    row = x * 128 + (z // 2) * 64 + y * 16
+                    for b in range(4):
+                        tile = e[*at, 0] if b == 0 else l[*at, b - 1]
+                        lo = b * 512 + position * 128
+                        gin[row : row + 16, lo : lo + 128] = tile.astype(F32) * factor
+                    row = position * 128 + (z // 2) * 64 + y * 16
+                    gout[row : row + 16, x * 128 : x * 128 + 128] = (
+                        e[*at, 1].astype(F32) * factor
+                    )
+        part = slice(x * 128, x * 128 + 128)
+        stores.append(
+            pltpu.make_async_copy(gin.at[part], gin_out.at[part], out_sem.at[x])
+        )
+        stores[-1].start()
+    for x in range(2):
+        part = slice(x * 256, x * 256 + 256)
+        stores.append(
+            pltpu.make_async_copy(gout.at[part], gout_out.at[part], out_sem.at[4 + x])
+        )
+        stores[-1].start()
+    for copy in rows_in:
+        copy.wait()
+    dxv[...] = (dxv[...].astype(F32) + dyv[...].astype(F32)).astype(BF)
+    stores.append(pltpu.make_async_copy(dxv, dx_out, out_sem.at[6]))
+    stores[-1].start()
+    for copy in stores:
+        copy.wait()
 
 
 def per_device(x_home, dy_home, w_in, w_out, place, seg_ids):
@@ -713,6 +756,7 @@
             vm((7, 2, 512, 512), BF),
             vm((7, 128, 512), F32),
             vm((4, 128, 512), F32),
+            vm((4, 128, 512), F32),
             vm((4, 4, 4, 512), F32),
             vm((4, 2, 128, 512), BF),
             vm((4, 512, 128), BF),
@@ -736,10 +780,10 @@
             vm((2, 512, 512), BF),
             vm((3, 2, 128, 512), BF),
             vm((2, 16, 16, 512), BF),
-            dma((6,)), dma((2,)), dma((2, 2)), dma((2, 3, 2)), dma((2, 3, 2)),
-            dma((2, 4, 2)), dma((2, 4, 2)), dma((2, 3)), dma((2, 3)), dma((2,)), dma((2,)),
-            dma((2, 4, 4)), dma((2, 4, 4)), dma((2,)), dma((2,)), dma((2,)),
-            dma((3, 2)), dma((3, 2)), dma((2,)),
+            dma((6,)), dma((2,)), dma((2, 2)), dma((2,)), dma((2, 3, 2)),
+            dma((2,)), dma((2, 4, 2)), dma((2,)), dma((2, 3)), dma((2,)), dma((2,)),
+            dma((2, 4)), dma((2, 2, 3)), dma((2,)), dma((2, 4, 3)), dma((2,)),
+            dma((1,)), dma((2,)), dma((1,)), dma((3, 2)), dma((2,)),
         ],
         compiler_params=pltpu.CompilerParams(
             collective_id=0, has_side_effects=True, vmem_limit_bytes=63 * 2**20
@@ -752,28 +796,27 @@
         place.reshape(1, 512),
         seg_ids.reshape(1, 2048),
     )
-    row = pl.BlockSpec((128, 512), lambda i: (i, 0))
-
-    def part(core, blocks):
-        if core == 0:
-            return pl.BlockSpec((1, 1, 4, 4, blocks, 16, 128), lambda i: (0, i, 0, 0, 0, 0, 0))
-        return pl.BlockSpec((1, 4, 1, 4, blocks, 16, 128), lambda i: (1, 0, i, 0, 0, 0, 0))
-
     return pl.pallas_call(
         finish_kernel,
-        grid=(4,),
         out_shape=(
             jax.ShapeDtypeStruct((512, 512), BF),
             jax.ShapeDtypeStruct((512, 2048), F32),
             jax.ShapeDtypeStruct((512, 512), F32),
         ),
-        in_specs=[row, row, part(0, 2), part(1, 2), part(0, 3), part(1, 3)],
-        out_specs=(
-            row,
-            pl.BlockSpec((128, 2048), lambda i: (i, 0)),
-            pl.BlockSpec((512, 128), lambda i: (0, i)),
-        ),
-    )(dx.reshape(512, 512), dy_home, early, early, late, late)
+        in_specs=[hbm, hbm, hbm, hbm],
+        out_specs=(hbm, hbm, hbm),
+        scratch_shapes=[
+            vm((2, 4, 4, 4, 2, 16, 128), BF),
+            vm((2, 4, 4, 4, 3, 16, 128), BF),
+            vm((512, 512), BF),
+            vm((512, 512), BF),
+            vm((512, 2048), F32),
+            vm((512, 512), F32),
+            dma((2, 9)),
+            dma((7,)),
+        ],
+        compiler_params=pltpu.CompilerParams(vmem_limit_bytes=62 * 2**20),
+    )(dx.reshape(512, 512), dy_home, early, late)
 
 
 def solution(mesh):

time: 105 us -> 102 us (0.971)
  Pallas kernels: 104 us -> 101 us
    pallas_call x1, Pallas kernels: 99.2 us -> 96.5 us  [per_device(): pl.pallas_call(kernel, out_shape=(jax.ShapeDtypeStruct(shape, BF), jax.Sh...]
where the time goes in v2:
time: 102 us
  Pallas kernels  101 us (99%)
    pallas_call x1, Pallas kernels, per_device(): pl.pallas_call(kernel, out_shape=(jax.ShapeDtypeStruct(shape, BF), jax.Sh...  96.5 us
    pallas_call x1, Pallas kernels, per_device(): pl.pallas_call(finish_kernel, out_shape=(jax.ShapeDtypeStruct((512, 512),...  4.29 us

profile of v2, /device:TPU:1, one launch (start us, length us, event | category | flops | bytes accessed | tf_op | source)
XLA Modules:
  0.0 101.6 jit_solution(14929252362014847517)
XLA Ops:
  0.6 96.5 %shard_map.85 = (bf16[4,2,4,16,512]{4,3,2,1,0:T(8,128)(2,1)}, bf16[2,4,4,4,2,16,128]{6,5,4,3,2,1,0:T(8,128)(2,1)}, bf16[2,4,4,4,3,16,128]{6,5,4,3,2,1,0:T(8,128)(2,1)}) custom-call(bf16[4,2,4,16,512]{4,3,2,1,0:T(8,128)(2,1)} %bitcast.5, bf16[4,2,4,16,512]{4,3,2,1,0:T(8,128)(2,1)} %bitcast.4, bf16[512,2048]{1,0:T(8,128)(2,1)} %win_ref.1, ...), custom_call_target="tpu_custom_call" | custom-call | tf_op jit(solution)/shard_map/pallas_call | solution.py:733
  97.1 4.3 %shard_map.86 = (bf16[512,512]{1,0:T(8,128)(2,1)}, f32[512,2048]{1,0:T(8,128)}, f32[512,512]{1,0:T(8,128)}) custom-call(bf16[512,512]{1,0:T(8,128)(2,1)} %bitcast.6, bf16[512,512]{1,0:T(8,128)(2,1)} %dy_ref.1, bf16[2,4,4,4,2,16,128]{6,5,4,3,2,1,0:T(8,128)(2,1)} %get-tuple-element.7.e_ref, bf16[2,4,4,4,3,16,128]{6,5,4,3,2,1,0:T(8,128)(2,1)} %get-tuple-element.8.l_ref), custom_call_target="tpu_custom_call" | custom-call | tf_op jit(solution)/shard_map/pallas_call | solution.py:799

commit v3 on v2

--- a/solution.py
+++ b/solution.py
@@ -380,12 +380,15 @@
         grad_u += mm(d_u, x_all[q])
 
     def grads_out(buf, got, sem):
-        @pl.loop(1, 16)
-        def _(i):
-            tx, ty = shifted(i, 1)
-            remote(
-                buf.at[tx, :, ty], got.at[i], sem.at[0], sem.at[1], (grp(tx, zl, ty), s)
-            ).start()
+        for low, high in ((8, 16), (1, 8)):
+
+            @pl.loop(low, high)
+            def _(i):
+                tx, ty = shifted(i, 1)
+                remote(
+                    buf.at[tx, :, ty], got.at[i], sem.at[0], sem.at[1],
+                    (grp(tx, zl, ty), s),
+                ).start()
 
         pltpu.make_async_copy(buf.at[x, :, y], got.at[0], sem.at[1]).start()
 
@@ -442,7 +445,7 @@
                 summed[t], piece(t, 0, 0),
                 ag_s.at[t, 1], ag_r.at[t, 1, i - 1], along(i, False),
             )
-            for i in range(1, 4)
+            for i in (2, 1, 3)
         ]
 
     def first_copies(t, i):
@@ -451,7 +454,7 @@
                 held(t, i), piece(t, i, 0),
                 ag_s.at[t, 2], first_r.at[t, i, j - 1], along(j, True),
             )
-            for j in range(1, 4)
+            for j in (2, 1, 3)
         ]
 
     def core_copy(t, i, j):
@@ -474,15 +477,15 @@
         own_copy(t).start()
 
     def gather_pass(t):
-        for i in range(1, 4):
+        for i in (1, 3, 2):
             wait_for(piece(t, i, 0), ag_r.at[t, 1, i - 1])
             for copy in first_copies(t, i):
                 copy.start()
             core_copy(t, i, 0).start()
 
     def gather_core(t):
-        for i in range(4):
-            for j in range(1, 4):
+        for i in (0, 1, 3, 2):
+            for j in (1, 3, 2):
                 wait_for(piece(t, i, j), first_r.at[t, i, j - 1])
                 core_copy(t, i, j).start()
 

time: 102 us -> 101 us (level)
  Pallas kernels: 101 us -> 99.9 us
where the time goes in v3:
time: 101 us
  Pallas kernels  99.9 us (99%)
    pallas_call x1, Pallas kernels, per_device(): pl.pallas_call(kernel, out_shape=(jax.ShapeDtypeStruct(shape, BF), jax.Sh...  95.6 us
    pallas_call x1, Pallas kernels, per_device(): pl.pallas_call(finish_kernel, out_shape=(jax.ShapeDtypeStruct((512, 512),...  4.29 us

profile of v3, /device:TPU:1, one launch (start us, length us, event | category | flops | bytes accessed | tf_op | source)
XLA Modules:
  0.0 100.7 jit_solution(12792348765154477662)
XLA Ops:
  0.6 95.6 %shard_map.85 = (bf16[4,2,4,16,512]{4,3,2,1,0:T(8,128)(2,1)}, bf16[2,4,4,4,2,16,128]{6,5,4,3,2,1,0:T(8,128)(2,1)}, bf16[2,4,4,4,3,16,128]{6,5,4,3,2,1,0:T(8,128)(2,1)}) custom-call(bf16[4,2,4,16,512]{4,3,2,1,0:T(8,128)(2,1)} %bitcast.5, bf16[4,2,4,16,512]{4,3,2,1,0:T(8,128)(2,1)} %bitcast.4, bf16[512,2048]{1,0:T(8,128)(2,1)} %win_ref.1, ...), custom_call_target="tpu_custom_call" | custom-call | tf_op jit(solution)/shard_map/pallas_call | solution.py:736
  96.3 4.3 %shard_map.86 = (bf16[512,512]{1,0:T(8,128)(2,1)}, f32[512,2048]{1,0:T(8,128)}, f32[512,512]{1,0:T(8,128)}) custom-call(bf16[512,512]{1,0:T(8,128)(2,1)} %bitcast.6, bf16[512,512]{1,0:T(8,128)(2,1)} %dy_ref.1, bf16[2,4,4,4,2,16,128]{6,5,4,3,2,1,0:T(8,128)(2,1)} %get-tuple-element.7.e_ref, bf16[2,4,4,4,3,16,128]{6,5,4,3,2,1,0:T(8,128)(2,1)} %get-tuple-element.8.l_ref), custom_call_target="tpu_custom_call" | custom-call | tf_op jit(solution)/shard_map/pallas_call | solution.py:802

commit v4 on v3

--- a/solution.py
+++ b/solution.py
@@ -417,7 +417,7 @@
     def meet(t):
         got, sem = reduced[t]
         wait_for(got, sem.at[1])
-        met[t][zz] = jnp.sum(got[...].astype(F32), axis=0)
+        met[t][zz] = jnp.sum(got[...].astype(F32), axis=0).astype(BF)
         for copy in z_copies(t):
             copy.start()
 
@@ -469,7 +469,7 @@
         for chunk in range(2):
             for to_zh in range(2):
                 summed[t][chunk * 2 + to_zh] = (
-                    met[t][to_zh, chunk] + met[t][2 + to_zh, chunk]
+                    met[t][to_zh, chunk].astype(F32) + met[t][2 + to_zh, chunk].astype(F32)
                 ).astype(BF)
         for copy in second_copies(t) + first_copies(t, 0):
             copy.start()
@@ -774,9 +774,9 @@
             vm((16, 2, 2, 16, 128), BF),
             vm((4, 2, 4, 3, 16, 128), BF),
             vm((16, 2, 3, 16, 128), BF),
-            vm((4, 2, 2, 16, 128), F32),
+            vm((4, 2, 2, 16, 128), BF),
             vm((4, 2, 16, 128), BF),
-            vm((4, 2, 3, 16, 128), F32),
+            vm((4, 2, 3, 16, 128), BF),
             vm((4, 3, 16, 128), BF),
             vm((384, 512), F32),
             vm((4, 512, 512), BF),

time: 101 us -> 99.5 us (0.985)
  Pallas kernels: 99.9 us -> 98.5 us
    pallas_call x1, Pallas kernels: 95.6 us -> 94.2 us  [per_device(): pl.pallas_call(kernel, out_shape=(jax.ShapeDtypeStruct(shape, BF), jax.Sh...]
where the time goes in v4:
time: 99.5 us; the launch traced here: 99.3 us
  Pallas kernels  98.5 us (99%)
    pallas_call x1, Pallas kernels, per_device(): pl.pallas_call(kernel, out_shape=(jax.ShapeDtypeStruct(shape, BF), jax.Sh...  94.2 us
    pallas_call x1, Pallas kernels, per_device(): pl.pallas_call(finish_kernel, out_shape=(jax.ShapeDtypeStruct((512, 512),...  4.29 us

profile of v4, /device:TPU:1, one launch (start us, length us, event | category | flops | bytes accessed | tf_op | source)
XLA Modules:
  0.0 99.3 jit_solution(137010796911298878)
XLA Ops:
  0.6 94.2 %shard_map.85 = (bf16[4,2,4,16,512]{4,3,2,1,0:T(8,128)(2,1)}, bf16[2,4,4,4,2,16,128]{6,5,4,3,2,1,0:T(8,128)(2,1)}, bf16[2,4,4,4,3,16,128]{6,5,4,3,2,1,0:T(8,128)(2,1)}) custom-call(bf16[4,2,4,16,512]{4,3,2,1,0:T(8,128)(2,1)} %bitcast.5, bf16[4,2,4,16,512]{4,3,2,1,0:T(8,128)(2,1)} %bitcast.4, bf16[512,2048]{1,0:T(8,128)(2,1)} %win_ref.1, ...), custom_call_target="tpu_custom_call" | custom-call | tf_op jit(solution)/shard_map/pallas_call | solution.py:736
  94.8 4.3 %shard_map.86 = (bf16[512,512]{1,0:T(8,128)(2,1)}, f32[512,2048]{1,0:T(8,128)}, f32[512,512]{1,0:T(8,128)}) custom-call(bf16[512,512]{1,0:T(8,128)(2,1)} %bitcast.6, bf16[512,512]{1,0:T(8,128)(2,1)} %dy_ref.1, bf16[2,4,4,4,2,16,128]{6,5,4,3,2,1,0:T(8,128)(2,1)} %get-tuple-element.7.e_ref, bf16[2,4,4,4,3,16,128]{6,5,4,3,2,1,0:T(8,128)(2,1)} %get-tuple-element.8.l_ref), custom_call_target="tpu_custom_call" | custom-call | tf_op jit(solution)/shard_map/pallas_call | solution.py:802
